TPU v7x, 512 devices: a whole 4x4x16 slice. The times are simulated.
512 devices in a mesh: row: 32 (over y_lo, z), col: 16 (over x, y_hi, core).
Axes of the slice: x: 4, y: 4 (y_hi: 2, y_lo: 2; y = y_hi * 2 + y_lo), z: 16, core: 2. Of those that a mesh axis runs over, the one named last changes fastest.
Arguments:
- bra_density: bfloat16 [8192, 12288], P('row', 'col'), may hold values from -6 to 6
- ket_density: bfloat16 [8192, 12288], P('col', 'row'), may hold values from -6 to 6
- coulomb: float32 [12288], replicated, may hold values from 0.002 to 0.02
- cond_pairs: bfloat16 [256, 8, 32, 256], P('row'), may hold values from -1 to 1
- val_pairs: bfloat16 [8, 32, 256, 256], P(None, None, 'col'), may hold values from -6 to 6
- screened: bfloat16 [16, 256, 256], P('col'), may hold values from -0.375 to 0.375
- q_owner: int32 [8, 8], replicated, may hold values from 0 to 15
- g_shift: int32 [8, 8, 256], replicated, may hold values from 0 to 255, each once within a row
Outputs:
- kernel: float32 [8192, 8192], P('row', 'col')
Inputs may be any that keep to these rules, and one draw needn't show every extreme that they name: `g_shift`: each row of the last dimension is a permutation of 0 to 255.
All inputs are finite; a program needn't handle non-finite values.
Results may differ from a plain program's by a relative error of at most 0.0029.
Values may be sent and summed in bfloat16 or wider, within the bound.
No kernel may reach another device: no remote copies, remote signals or barrier semaphores. Data moves between devices by JAX's collectives and lax.ppermute only.
A program may use at most 64 MiB of HBM per device.

v0:
```python
import jax
import jax.numpy as jnp
from jax import lax
from jax.sharding import PartitionSpec as P


def local(bra_density, ket_density, coulomb, cond_pairs, val_pairs, screened, q_owner, g_shift):
    bra_index = lax.axis_index("row")
    ket_index = lax.axis_index("col")
    cb_size = cond_pairs.shape[0]
    nc_size = cond_pairs.shape[2]
    nv_size = val_pairs.shape[1]
    vb_size = val_pairs.shape[2]
    ngw_size = val_pairs.shape[3]
    kbra = bra_index // (nc_size // cb_size)
    kket = ket_index // (nv_size // vb_size)
    ket_all = lax.all_gather(ket_density, "row", axis=1, tiled=True)
    scaled = (
        lax.all_gather(bra_density, "col", axis=1, tiled=True).astype(jnp.float32)
        * coulomb[None, :]
    ).astype(jnp.bfloat16)
    exchange = lax.dot_general(
        scaled, ket_all, (((1,), (1,)), ((), ())), preferred_element_type=jnp.float32
    )
    q_index = q_owner[kbra, kket]
    perm = g_shift[kbra, kket]
    vals = lax.dynamic_index_in_dim(val_pairs, kbra, 0, keepdims=False)
    shifted = jnp.take(vals, perm, axis=2).reshape(nv_size * vb_size, ngw_size)
    blocks = lax.all_gather(screened, "col", axis=0, tiled=True)
    w_block = lax.dynamic_index_in_dim(blocks, q_index, 0, keepdims=False)
    pairs = lax.dot_general(
        shifted, w_block, (((1,), (1,)), ((), ())), preferred_element_type=jnp.float32
    )
    pairs = pairs.astype(jnp.bfloat16).reshape(nv_size, vb_size, ngw_size)
    conds = lax.dynamic_index_in_dim(cond_pairs, kket, 1, keepdims=False)
    direct = jnp.einsum("xcg,vug->vxuc", conds, pairs, preferred_element_type=jnp.float32)
    direct = direct.reshape(nv_size * cb_size, vb_size * nc_size)
    return 2.0 * exchange - direct


def solution(mesh):
    return jax.shard_map(
        local,
        mesh=mesh,
        in_specs=(
            P("row", "col"),
            P("col", "row"),
            P(),
            P("row", None, None, None),
            P(None, None, "col", None),
            P("col", None, None),
            P(),
            P(),
        ),
        out_specs=P("row", "col"),
        check_vma=False,
    )
```

profile of v0, /device:TPU:6, one launch (start us, length us, event | category | flops | bytes accessed | tf_op | source)
XLA Modules:
  0.0 340.2 jit_solution(5203356275561595495)
XLA Ops:
  6.5 0.0 copy-start
  6.5 0.0 copy-start.1
  6.5 0.0 all-gather.8.cloned.1.call-start
  6.5 0.7 all-gather.8.cloned.1.call-update
  7.3 0.0 all-gather.4.cloned.1.call-start
  7.3 0.7 all-gather.4.cloned.1.call-update
  8.0 0.0 all-gather.6.cloned.1.call-start
  8.1 0.7 all-gather.6.cloned.1.call-update
  8.8 0.0 copy-done
  8.8 1.0 copy.12
  9.9 0.7 compare_select_fusion
  10.6 1.8 gather_fusion
  12.4 2.0 select_bitcast_fusion
  14.3 1.1 copy.13
  15.4 1.3 dynamic_slice.20
  18.6 60.0 %all-gather.8.cloned.1.call-done = bf16[16,256,256]{2,1,0:T(8,128)(2,1)} async-done(((bf16[1,256,256]{2,1,0:T(8,128)(2,1)}), bf16[16,256,256]{2,1,0:T(8,128)(2,1)}) %all-gather.8.cloned.1.call-update) | async-done | bytes 2097168 | tf_op jit(solution)/shard_map/all_gather | solution.py:29
  78.6 1.2 convolution_convert_fusion
  79.8 2.7 convolution_bitcast_fusion
  82.4 2.3 reshape.67
  84.7 74.6 %all-gather.4.cloned.1.call-done = bf16[256,12288]{1,0:T(8,128)(2,1)} async-done(((bf16[256,768]{1,0:T(8,128)(2,1)}), bf16[256,12288]{1,0:T(8,128)(2,1)}) %all-gather.4.cloned.1.call-update) | async-done | bytes 6291472 | tf_op jit(solution)/shard_map/all_gather | solution.py:19
  159.4 163.7 %all-gather.6.cloned.1.call-done = bf16[512,12288]{1,0:T(8,128)(2,1)} async-done(((bf16[512,384]{1,0:T(8,128)(2,1)}), bf16[512,12288]{1,0:T(8,128)(2,1)}) %all-gather.6.cloned.1.call-update) | async-done | bytes 12582928 | tf_op jit(solution)/shard_map/all_gather | solution.py:17
  323.0 0.0 copy-done.1
  323.1 10.6 %fusion.3 = f32[256,512]{1,0:T(8,128)} fusion(f32[256,512]{1,0:T(8,128)S(1)} %reshape.67, bf16[512,12288]{1,0:T(8,128)(2,1)} %all-gather.6.cloned.1.call-done, bf16[256,12288]{1,0:T(8,128)(2,1)} %all-gather.4.cloned.1.call-done, f32[12288]{0:T(1024)S(1)} %copy-done.1), kind=kOutput, calls=%fused_computation.6 | convolution fusion | flops 3230924800 | bytes 19972096 | tf_op jit(solution)/shard_map/dot_general | solution.py:22
  (3 shorter events, 0.0 us)
Async XLA Ops:
  6.5 2.2 copy-start
  6.5 316.5 %copy-start.1 = (f32[12288]{0:T(1024)S(1)}, f32[12288]{0:T(1024)}, u32[]{:S(2)}) copy-start(f32[12288]{0:T(1024)} %param.10) | copy-start | bytes 147460
  6.5 72.1 %all-gather.8.cloned.1.call-start = ((), (), s32[]{:S(2)}) async-start(), calls=%async_computation.2 | async-start | bytes 2228224 | tf_op jit(solution)/shard_map/all_gather | solution.py:29
  7.3 152.1 %all-gather.4.cloned.1.call-start = ((), (), s32[]{:S(2)}) async-start(), calls=%async_computation | async-start | bytes 6684672 | tf_op jit(solution)/shard_map/all_gather | solution.py:19
  8.0 315.0 %all-gather.6.cloned.1.call-start = ((), (), s32[]{:S(2)}) async-start(), calls=%async_computation.1 | async-start | bytes 12976128 | tf_op jit(solution)/shard_map/all_gather | solution.py:17
Sparse Core Ops, SparseCore 0:
  10.6 67.9 all-gather.7
  81.9 77.4 all-gather.3
  161.5 161.5 all-gather.5
where the time goes:
time: 340 us
  waiting for transfers between devices  300 us (88%)
  between operations  15.1 us (4%)
  matrix products  14.5 us (4%)
  local copies, waits for them, and re-layouts  7.5 us (2%)
    all_gather x1, waiting for transfers between devices, local(): ket_all = lax.all_gather(ket_density, 'row', axis=1, tiled=True)  164 us
    all_gather x1, waiting for transfers between devices, local(): lax.all_gather(bra_density, 'col', axis=1, tiled=True).astype(jnp.float32)  74.6 us
    all_gather x1, waiting for transfers between devices, local(): blocks = lax.all_gather(screened, 'col', axis=0, tiled=True)  60 us
    dot_general x1, matrix products, local(): lax.dot_general(scaled, ket_all, (((1,), (1,)), ((), ())), preferred_elem...  10.6 us
  transfers between devices with their start and end apart: 3, of which 3 were waited for; matrix products, arithmetic and copies ran while one was open for 4% of the time, Pallas kernels for 0%

commit v1 on v0

v1 whole, which is shorter than its diff:
```python
import jax
import jax.numpy as jnp
from jax import lax
from jax.experimental import pallas as pl
from jax.experimental.pallas import tpu as pltpu
from jax.sharding import Mesh, PartitionSpec as P

AXES = ("ylo", "z", "x", "yhi", "core")
SIZES = (2, 16, 4, 2, 2)
ROW = ("ylo", "z")
COL = ("x", "yhi", "core")


def flat(place):
    index = 0
    for at, size in zip(place, SIZES):
        index = index * size + at
    return index


def permute(array, target):
    pairs = []
    for ylo in range(2):
        for z in range(16):
            for x in range(4):
                for yhi in range(2):
                    for core in range(2):
                        place = (ylo, z, x, yhi, core)
                        pairs.append((flat(place), flat(target(*place))))
    return lax.ppermute(array, AXES, pairs)


def product_t(a, b):
    return lax.dot_general(a, b, (((1,), (1,)), ((), ())), preferred_element_type=jnp.float32)


def sum_kernel(where, mine, other, ket, *refs):
    minus, (out, bras, kets, total, arrived) = (refs[0] if len(refs) == 6 else None), refs[-5:]
    width = ket.shape[2]
    first, core = where[0], where[1]
    copies = []
    for n in range(8):
        source, h = ((mine, core), (other, 1 - core))[n % 2]
        j = n // 2
        copies.append(
            (
                pltpu.make_async_copy(
                    source.at[first + j, :, pl.ds(0, 2 * width)], bras.at[n], arrived.at[0, n]
                ),
                pltpu.make_async_copy(ket.at[pl.ds(4 * j + 2 * h, 2)], kets.at[n], arrived.at[1, n]),
            )
        )
    for pair in copies:
        for copy in pair:
            copy.start()
    for n, pair in enumerate(copies):
        for copy in pair:
            copy.wait()
        part = product_t(bras[n, :, :width], kets[n, 0])
        part = part + product_t(bras[n, :, width:], kets[n, 1])
        if n > 0:
            total[...] += part
        elif minus is None:
            total[...] = part
        else:
            total[...] = part - minus[...]
    out[...] = total[...].astype(out.dtype)


def partial_sum(mine, other, ket, group, core, dtype, minus=None):
    rows, (blocks, columns, width) = mine.shape[1], ket.shape
    where = jnp.stack([group * 4, core]).astype(jnp.int32)
    inside = pl.BlockSpec(memory_space=pltpu.VMEM)
    outside = pl.BlockSpec(memory_space=pltpu.HBM)
    more = () if minus is None else (minus,)
    return pl.pallas_call(
        sum_kernel,
        out_shape=jax.ShapeDtypeStruct((rows, columns), dtype),
        in_specs=[pl.BlockSpec(memory_space=pltpu.SMEM)] + [outside] * 3 + [inside] * len(more),
        out_specs=inside,
        scratch_shapes=[
            pltpu.VMEM((8, rows, 2 * width), mine.dtype),
            pltpu.VMEM((8, 2, columns, width), ket.dtype),
            pltpu.VMEM((rows, columns), jnp.float32),
            pltpu.SemaphoreType.DMA((2, 8)),
        ],
        compiler_params=pltpu.CompilerParams(vmem_limit_bytes=56 * 1024 * 1024),
        cost_estimate=pl.CostEstimate(
            flops=2 * rows * columns * blocks * width,
            bytes_accessed=2 * (rows + columns) * blocks * width,
            transcendentals=0,
        ),
    )(where, mine, other, ket, *more)


def local(bra_density, ket_density, coulomb, cond_pairs, val_pairs, screened, q_owner, g_shift):
    ylo = lax.axis_index("ylo")
    z = lax.axis_index("z")
    core = lax.axis_index("core")
    bra_index = lax.axis_index(ROW)
    ket_index = lax.axis_index(COL)
    cb_size = cond_pairs.shape[0]
    nc_size = cond_pairs.shape[2]
    nv_size = val_pairs.shape[1]
    vb_size = val_pairs.shape[2]
    ngw_size = val_pairs.shape[3]
    kbra = bra_index // (nc_size // cb_size)
    kket = ket_index // (nv_size // vb_size)
    rows, chunk = bra_density.shape
    half = ngw_size // 2

    ket = lax.all_gather(ket_density, "z", axis=0)

    gains = lax.dynamic_slice_in_dim(coulomb, ket_index * chunk, chunk)
    scaled = (bra_density.astype(jnp.float32) * gains[None, :]).astype(jnp.bfloat16) * 2
    moved = permute(scaled, lambda yl, zz, x, yh, c: (x // 2, zz, yl * 2 + x % 2, yh, c))

    q_index = q_owner[kbra, kket]
    w_half = lax.dynamic_slice_in_dim(screened[0], (z % 2) * half, half, 1)
    w_all = lax.all_to_all(
        jnp.broadcast_to(w_half[None], (8,) + w_half.shape), ("x", "yhi"), 0, 0, tiled=True
    )
    w_mine = lax.dynamic_index_in_dim(w_all, q_index // 2, 0, keepdims=False)
    w_other = permute(w_mine, lambda yl, zz, x, yh, c: (yl, zz, x, yh, 1 - c))
    w_mine = jnp.where(q_index % 2 == core, w_mine, w_other)
    w_other = permute(w_mine, lambda yl, zz, x, yh, c: (yl, zz ^ 1, x, yh, c))

    moved, w_mine = lax.optimization_barrier((moved, w_mine))
    spread = jnp.broadcast_to(moved[None], (8,) + moved.shape)
    mine = lax.all_to_all(spread, ("x", "yhi"), 0, 0, tiled=True)
    other = permute(mine, lambda yl, zz, x, yh, c: (yl, zz, x, yh, 1 - c))
    w_mine, w_other, val_pairs, cond_pairs, mine = lax.optimization_barrier(
        (w_mine, w_other, val_pairs, cond_pairs, mine)
    )
    w_block = jnp.concatenate(
        [jnp.where(z % 2 == 0, w_mine, w_other), jnp.where(z % 2 == 0, w_other, w_mine)], axis=1
    )
    perm = g_shift[kbra, kket]
    vals = lax.dynamic_index_in_dim(val_pairs, kbra, 0, keepdims=False)
    shifted = jnp.take(vals, perm, axis=2).reshape(nv_size * vb_size, ngw_size)
    pairs = lax.dot_general(
        shifted, w_block, (((1,), (1,)), ((), ())), preferred_element_type=jnp.float32
    )
    pairs = pairs.astype(jnp.bfloat16).reshape(nv_size, vb_size, ngw_size)
    conds = lax.dynamic_index_in_dim(cond_pairs, kket, 1, keepdims=False)
    direct = jnp.einsum("xcg,vug->vxuc", conds, pairs, preferred_element_type=jnp.float32)

    direct = direct.reshape(nv_size * cb_size, vb_size * nc_size)
    direct, ket = lax.optimization_barrier((direct, ket))
    send = partial_sum(mine, other, ket, 1 - ylo, core, jnp.bfloat16)
    got = permute(send, lambda yl, zz, x, yh, c: (1 - yl, zz, x, yh, c))
    keep = partial_sum(mine, other, ket, ylo, core, jnp.float32, direct)
    return keep + got.astype(jnp.float32)


def solution(mesh):
    fine = Mesh(mesh.devices.reshape(SIZES), AXES)
    return jax.shard_map(
        local,
        mesh=fine,
        in_specs=(
            P(ROW, COL),
            P(COL, ROW),
            P(),
            P(ROW, None, None, None),
            P(None, None, COL, None),
            P(COL, None, None),
            P(),
            P(),
        ),
        out_specs=P(ROW, COL),
        check_vma=False,
    )
```

time: 340 us -> 127 us (0.37)
  waiting for transfers between devices: 300 us -> 12.3 us
  blocking collectives: 0 us -> 42.4 us
  starting transfers between devices: 0.08 us -> 23.8 us
  Pallas kernels: 0 us -> 12 us
  matrix products: 14.5 us -> 2.96 us
  local copies, waits for them, and re-layouts: 7.5 us -> 12.3 us
    all_gather x3 -> x1, waiting for transfers between devices: 298 us -> 3.12 us  [local(): ket = lax.all_gather(ket_density, 'z', axis=0)]
    all_to_all x0 -> x1, blocking collectives: none -> 42.4 us  [local(): mine = lax.all_to_all(spread, ('x', 'yhi'), 0, 0, tiled=True)]
    ppermute x0 -> x5, starting transfers between devices: none -> 14.5 us  [permute(): return lax.ppermute(array, AXES, pairs)]
    pallas_call x0 -> x2, Pallas kernels: none -> 12 us  [partial_sum(): pl.pallas_call(sum_kernel, out_shape=jax.ShapeDtypeStruct((rows, columns)...]
    dot_general x1 -> x0, matrix products: 10.6 us -> none  [local(): lax.dot_general(scaled, ket_all, (((1,), (1,)), ((), ())), preferred_elem...]
    all_to_all x0 -> x1, starting transfers between devices: none -> 9.28 us  [local(): lax.all_to_all(jnp.broadcast_to(w_half[None], (8,) + w_half.shape), ('x',...]
    ppermute x0 -> x5, waiting for transfers between devices: none -> 6.51 us  [permute(): return lax.ppermute(array, AXES, pairs)]
  transfers between devices with their start and end apart: 3 -> 7, of which waited for: 3 -> 5; matrix products, arithmetic and copies ran while one was open for 4% -> 14% of each run, Pallas kernels for 0% -> 5%
where the time goes in v1:
time: 127 us; the launch traced here: 126 us
  blocking collectives  42.4 us (33%)
  starting transfers between devices  23.8 us (19%)
  between operations  16.4 us (13%)
  local copies, waits for them, and re-layouts  12.3 us (10%)
  waiting for transfers between devices  12.3 us (10%)
  Pallas kernels  12 us (9%)
  other arithmetic  4.06 us (3%)
  matrix products  2.96 us (2%)
    all_to_all x1, blocking collectives, local(): mine = lax.all_to_all(spread, ('x', 'yhi'), 0, 0, tiled=True)  42.4 us
    ppermute x5, starting transfers between devices, permute(): return lax.ppermute(array, AXES, pairs)  14.5 us
    pallas_call x2, Pallas kernels, partial_sum(): pl.pallas_call(sum_kernel, out_shape=jax.ShapeDtypeStruct((rows, columns)...  12 us
    all_to_all x1, starting transfers between devices, local(): lax.all_to_all(jnp.broadcast_to(w_half[None], (8,) + w_half.shape), ('x',...  9.28 us
    ppermute x5, waiting for transfers between devices, permute(): return lax.ppermute(array, AXES, pairs)  6.51 us
    gather x2, local copies, waits for them, and re-layouts, local(): shifted = jnp.take(vals, perm, axis=2).reshape(nv_size * vb_size, ngw_size)  4.25 us
    all_gather x1, waiting for transfers between devices, local(): ket = lax.all_gather(ket_density, 'z', axis=0)  3.12 us
    reshape x1, local copies, waits for them, and re-layouts, local(): direct = direct.reshape(nv_size * cb_size, vb_size * nc_size)  2.96 us
  transfers between devices with their start and end apart: 7, of which 5 were waited for; matrix products, arithmetic and copies ran while one was open for 14% of the time, Pallas kernels for 5%

profile of v1, /device:TPU:6, one launch (start us, length us, event | category | flops | bytes accessed | tf_op | source)
XLA Modules:
  0.0 126.3 jit_solution(18232294241595562585)
XLA Ops:
  7.3 0.8 dynamic-slice_bitcast_fusion.1
  8.1 0.9 broadcast_in_dim.26
  9.0 9.3 %all-to-all-start = ((bf16[8,256,128]{2,1,0:T(8,128)(2,1)}), bf16[8,256,128]{2,1,0:T(8,128)(2,1)S(1)}, u32[]{:S(2)}, u32[]{:S(2)}) async-start(bf16[8,256,128]{2,1,0:T(8,128)(2,1)} %broadcast_in_dim.26), calls=%async_computation | async-start | bytes 1048576 | tf_op jit(solution)/shard_map/all_to_all | solution.py:120
  18.3 0.8 dynamic_slice.24
  19.1 1.9 %collective-permute-start = (bf16[256,768]{1,0:T(8,128)(2,1)S(1)}, bf16[256,768]{1,0:T(8,128)(2,1)S(1)}, u32[]{:S(2)}, u32[]{:S(2)}) collective-permute-start(bf16[256,768]{1,0:T(8,128)(2,1)S(1)} %fusion), channel_id=1, source_target_pairs={{0,0},{1,1},{2,2},{3,3},{4,4},{5,5},{6,6},{7,7},{8,256},{9,257},{1... | collective-permute-start | bytes 1179656 | tf_op jit(solution)/shard_map/ppermute | solution.py:30
  21.1 1.4 %dynamic_slice.25 = s32[1,1]{1,0:T(1,128)} dynamic-slice(s32[8,8]{1,0:T(8,128)} %param.14, s32[]{:T(128)S(6)} %select_n.88, s32[]{:T(128)S(6)} %select_n.90), dynamic_slice_sizes={1,1} | dynamic-slice | bytes 12 | tf_op jit(solution)/shard_map/dynamic_slice | solution.py:118
  25.3 2.0 %all-to-all-done = bf16[8,256,128]{2,1,0:T(8,128)(2,1)S(1)} async-done(((bf16[8,256,128]{2,1,0:T(8,128)(2,1)}), bf16[8,256,128]{2,1,0:T(8,128)(2,1)S(1)}, u32[]{:S(2)}, u32[]{:S(2)}) %all-to-all-start) | async-done | bytes 524320 | tf_op jit(solution)/shard_map/all_to_all | solution.py:120
  27.3 1.9 %collective-permute-start.1 = (bf16[256,128]{1,0:T(8,128)(2,1)S(1)}, bf16[256,128]{1,0:T(8,128)(2,1)S(1)}, u32[]{:S(2)}, u32[]{:S(2)}) collective-permute-start(bf16[256,128]{1,0:T(8,128)(2,1)S(1)} %dynamic-slice_bitcast_fusion), channel_id=1, source_target_pairs={{0,1},{1,0},{2,3},{3,2},{4,5},{5,4},{6,7},{7,6},{8,9},{9,8},{10,11... | collective-permute-start | bytes 196616 | tf_op jit(solution)/shard_map/ppermute | solution.py:30
  29.2 1.2 collective-permute-done.1
  30.4 1.9 %collective-permute-done = bf16[256,768]{1,0:T(8,128)(2,1)S(1)} collective-permute-done((bf16[256,768]{1,0:T(8,128)(2,1)S(1)}, bf16[256,768]{1,0:T(8,128)(2,1)S(1)}, u32[]{:S(2)}, u32[]{:S(2)}) %collective-permute-start) | collective-permute-done | bytes 393248 | tf_op jit(solution)/shard_map/ppermute | solution.py:30
  32.6 42.4 %all_to_all.10.mine = bf16[8,256,768]{2,1,0:T(8,128)(2,1)} all-to-all(bf16[8,256,768]{2,1,0:T(8,128)(2,1)S(1)} %broadcast_in_dim.27), channel_id=1, replica_groups=mesh['ylo'=2,'z'=16,'x'=4,'yhi'=2,'core'=2] {'x','yhi'}, dimensions={0} | all-to-all | bytes 6291456 | tf_op jit(solution)/shard_map/all_to_all | solution.py:130
  74.9 1.9 %collective-permute-start.3 = (bf16[8,256,768]{2,1,0:T(8,128)(2,1)}, bf16[8,256,768]{2,1,0:T(8,128)(2,1)}, u32[]{:S(2)}, u32[]{:S(2)}) collective-permute-start(bf16[8,256,768]{2,1,0:T(8,128)(2,1)} %all_to_all.10.mine), channel_id=1, source_target_pairs={{0,1},{1,0},{2,3},{3,2},{4,5},{5,4},{6,7},{7,6},{8,9},{9,8},{10,11... | collective-permute-start | bytes 9437192 | tf_op jit(solution)/shard_map/ppermute | solution.py:30
  77.6 5.3 %collective-permute-start.2 = (bf16[256,128]{1,0:T(8,128)(2,1)S(1)}, bf16[256,128]{1,0:T(8,128)(2,1)S(1)}, u32[]{:S(2)}, u32[]{:S(2)}) collective-permute-start(bf16[256,128]{1,0:T(8,128)(2,1)S(1)} %broadcast_select_fusion.2), channel_id=1, source_target_pairs={{0,16},{1,17},{2,18},{3,19},{4,20},{5,21},{6,22},{7,23},{8,24},{9,... | collective-permute-start | bytes 196616 | tf_op jit(solution)/shard_map/ppermute | solution.py:30
  83.6 3.4 %collective-permute-done.2 = bf16[256,128]{1,0:T(8,128)(2,1)S(1)} collective-permute-done((bf16[256,128]{1,0:T(8,128)(2,1)S(1)}, bf16[256,128]{1,0:T(8,128)(2,1)S(1)}, u32[]{:S(2)}, u32[]{:S(2)}) %collective-permute-start.2) | collective-permute-done | bytes 65568 | tf_op jit(solution)/shard_map/ppermute | solution.py:30
  87.0 1.0 copy.10
  88.0 1.8 %gather_fusion = bf16[256,32,16]{1,2,0:T(8,128)(2,1)} fusion(bf16[32,16,256]{0,1,2:T(8,128)(2,1)S(1)} %bitcast.36, s32[1024]{0:T(1024)S(1)} %pad_clamp_fusion), kind=kCustom, calls=%fused_computation | custom fusion | bytes 525312 | tf_op jit(solution)/shard_map/jit(_take)/gather | solution.py:140
  89.9 2.4 %copy.11 = bf16[32,16,256]{2,1,0:T(8,128)(2,1)S(1)} copy(bf16[32,16,256]{0,1,2:T(8,128)(2,1)} %bitcast.37) | data formatting | bytes 524288 | tf_op jit(solution)/shard_map/jit(_take)/gather | solution.py:140
  92.6 2.7 %convolution_bitcast_fusion = f32[32,8,16,32]{3,2,1,0:T(8,128)} fusion(bf16[32,16,256,1]{2,1,3,0:T(8,128)(2,1)S(1)} %bitcast.38, bf16[8,8,32,256]{3,2,1,0:T(8,128)(2,1)} %param.11, s32[]{:T(128)S(6)} %select_n.90), kind=kOutput, calls=%fused_computation.1 | convolution fusion | flops 67108864 | bytes 917508 | tf_op jit(solution)/shard_map/xcg,vug->vxuc/dot_general | solution.py:146
  95.3 3.0 %reshape.47.refs_0_ = f32[256,512]{1,0:T(8,128)} reshape(f32[32,8,16,32]{3,2,1,0:T(8,128)} %convolution_bitcast_fusion) | data formatting | bytes 1048576 | tf_op jit(solution)/shard_map/reshape | solution.py:148
  98.3 3.1 %all-gather.3.cloned.1.call-done = bf16[8192,384]{1,0:T(8,128)(2,1)} async-done(((bf16[512,384]{1,0:T(8,128)(2,1)}), bf16[8192,384]{1,0:T(8,128)(2,1)}) %all-gather.3.cloned.1.call-update) | async-done | bytes 6291472 | tf_op jit(solution)/shard_map/all_gather | solution.py:112
  101.4 5.7 %shard_map.83 = bf16[256,512]{1,0:T(8,128)(2,1)} custom-call(s32[2]{0:T(128)} %pad_add_fusion.1.where, bf16[8,256,768]{2,1,0:T(8,128)(2,1)} %all_to_all.10.mine, bf16[8,256,768]{2,1,0:T(8,128)(2,1)} %collective-permute-done.3.other, bf16[16,512,384]{2,1,0:T(8,128)(2,1)} %bitcast.34), custom_call_target="tpu_custom_call" | custom-call | flops 1610612736 | bytes 9437184 | tf_op jit(solution)/shard_map/pallas_call | solution.py:76
  107.1 3.4 %collective-permute-start.4 = (bf16[256,512]{1,0:T(8,128)(2,1)}, bf16[256,512]{1,0:T(8,128)(2,1)S(1)}, u32[]{:S(2)}, u32[]{:S(2)}) collective-permute-start(bf16[256,512]{1,0:T(8,128)(2,1)} %shard_map.83), channel_id=1, source_target_pairs={{0,256},{1,257},{2,258},{3,259},{4,260},{5,261},{6,262},{7,263},{8... | collective-permute-start | bytes 786440 | tf_op jit(solution)/shard_map/ppermute | solution.py:30
  111.2 6.3 %shard_map.82 = f32[256,512]{1,0:T(8,128)} custom-call(s32[2]{0:T(128)} %pad_add_fusion.where, bf16[8,256,768]{2,1,0:T(8,128)(2,1)} %all_to_all.10.mine, bf16[8,256,768]{2,1,0:T(8,128)(2,1)} %collective-permute-done.3.other, bf16[16,512,384]{2,1,0:T(8,128)(2,1)} %bitcast.35, f32[256,512]{1,0:T(8,128)} %reshape.47.refs_0_), custom_call_target="tpu_custom_call" | custom-call | flops 1610612736 | bytes 9437184 | tf_op jit(solution)/shard_map/pallas_call | solution.py:76
  117.5 1.9 %convert_add_fusion = f32[256,512]{1,0:T(8,128)} fusion(f32[256,512]{1,0:T(8,128)} %shard_map.82, bf16[256,512]{1,0:T(8,128)(2,1)S(1)} %collective-permute-done.4), kind=kLoop, calls=%fused_computation.4 | loop fusion | flops 262144 | bytes 1310720 | tf_op jit(solution)/shard_map/add | solution.py:153
  (21 shorter events, 3.4 us)
Async XLA Ops:
  6.5 80.4 %copy-start = (bf16[8,32,16,256]{3,2,1,0:T(8,128)(2,1)S(1)}, bf16[8,32,16,256]{3,2,1,0:T(8,128)(2,1)}, u32[]{:S(2)}) copy-start(bf16[8,32,16,256]{3,2,1,0:T(8,128)(2,1)} %param.12) | copy-start | bytes 6291460
  6.5 12.5 %copy-start.1 = (bf16[256,768]{1,0:T(8,128)(2,1)S(1)}, bf16[256,768]{1,0:T(8,128)(2,1)}, u32[]{:S(2)}) copy-start(bf16[256,768]{1,0:T(8,128)(2,1)} %param.8) | copy-start | bytes 1179652
  6.5 94.9 %all-gather.3.cloned.1.call-start = ((), (), s32[]{:S(2)}) async-start(), calls=%async_computation.2 | async-start | bytes 6684672 | tf_op jit(solution)/shard_map/all_gather | solution.py:112
  9.0 18.3 %all-to-all-start = ((bf16[8,256,128]{2,1,0:T(8,128)(2,1)}), bf16[8,256,128]{2,1,0:T(8,128)(2,1)S(1)}, u32[]{:S(2)}, u32[]{:S(2)}) async-start(bf16[8,256,128]{2,1,0:T(8,128)(2,1)} %broadcast_in_dim.26), calls=%async_computation | async-start | bytes 1048576 | tf_op jit(solution)/shard_map/all_to_all | solution.py:120
  19.1 13.2 %collective-permute-start = (bf16[256,768]{1,0:T(8,128)(2,1)S(1)}, bf16[256,768]{1,0:T(8,128)(2,1)S(1)}, u32[]{:S(2)}, u32[]{:S(2)}) collective-permute-start(bf16[256,768]{1,0:T(8,128)(2,1)S(1)} %fusion), channel_id=1, source_target_pairs={{0,0},{1,1},{2,2},{3,3},{4,4},{5,5},{6,6},{7,7},{8,256},{9,257},{1... | collective-permute-start | bytes 1179656 | tf_op jit(solution)/shard_map/ppermute | solution.py:30
  27.3 3.1 %collective-permute-start.1 = (bf16[256,128]{1,0:T(8,128)(2,1)S(1)}, bf16[256,128]{1,0:T(8,128)(2,1)S(1)}, u32[]{:S(2)}, u32[]{:S(2)}) collective-permute-start(bf16[256,128]{1,0:T(8,128)(2,1)S(1)} %dynamic-slice_bitcast_fusion), channel_id=1, source_target_pairs={{0,1},{1,0},{2,3},{3,2},{4,5},{5,4},{6,7},{7,6},{8,9},{9,8},{10,11... | collective-permute-start | bytes 196616 | tf_op jit(solution)/shard_map/ppermute | solution.py:30
  74.9 26.5 %collective-permute-start.3 = (bf16[8,256,768]{2,1,0:T(8,128)(2,1)}, bf16[8,256,768]{2,1,0:T(8,128)(2,1)}, u32[]{:S(2)}, u32[]{:S(2)}) collective-permute-start(bf16[8,256,768]{2,1,0:T(8,128)(2,1)} %all_to_all.10.mine), channel_id=1, source_target_pairs={{0,1},{1,0},{2,3},{3,2},{4,5},{5,4},{6,7},{7,6},{8,9},{9,8},{10,11... | collective-permute-start | bytes 9437192 | tf_op jit(solution)/shard_map/ppermute | solution.py:30
  77.6 9.4 %collective-permute-start.2 = (bf16[256,128]{1,0:T(8,128)(2,1)S(1)}, bf16[256,128]{1,0:T(8,128)(2,1)S(1)}, u32[]{:S(2)}, u32[]{:S(2)}) collective-permute-start(bf16[256,128]{1,0:T(8,128)(2,1)S(1)} %broadcast_select_fusion.2), channel_id=1, source_target_pairs={{0,16},{1,17},{2,18},{3,19},{4,20},{5,21},{6,22},{7,23},{8,24},{9,... | collective-permute-start | bytes 196616 | tf_op jit(solution)/shard_map/ppermute | solution.py:30
  107.1 10.4 %collective-permute-start.4 = (bf16[256,512]{1,0:T(8,128)(2,1)}, bf16[256,512]{1,0:T(8,128)(2,1)S(1)}, u32[]{:S(2)}, u32[]{:S(2)}) collective-permute-start(bf16[256,512]{1,0:T(8,128)(2,1)} %shard_map.83), channel_id=1, source_target_pairs={{0,256},{1,257},{2,258},{3,259},{4,260},{5,261},{6,262},{7,263},{8... | collective-permute-start | bytes 786440 | tf_op jit(solution)/shard_map/ppermute | solution.py:30
Sparse Core Ops, SparseCore 0:
  9.4 91.9 all-gather.2

commit v2 on v1

--- a/solution.py
+++ b/solution.py
@@ -1,3 +1,5 @@
+import functools
+
 import jax
 import jax.numpy as jnp
 from jax import lax
@@ -34,10 +36,13 @@
     return lax.dot_general(a, b, (((1,), (1,)), ((), ())), preferred_element_type=jnp.float32)
 
 
-def sum_kernel(where, mine, other, ket, *refs):
-    minus, (out, bras, kets, total, arrived) = (refs[0] if len(refs) == 6 else None), refs[-5:]
+def sum_kernel(turn, where, mine, other, ket, *refs):
     width = ket.shape[2]
-    first, core = where[0], where[1]
+    first, core = where[turn], where[2]
+    if turn == 0:
+        out, bras, kets, total, arrived = refs
+    else:
+        minus, out, bras, kets, total, arrived, less, less_arrived = refs
     copies = []
     for n in range(8):
         source, h = ((mine, core), (other, 1 - core))[n % 2]
@@ -53,44 +58,50 @@
     for pair in copies:
         for copy in pair:
             copy.start()
+    if turn == 1:
+        last = pltpu.make_async_copy(minus, less, less_arrived)
+        last.start()
     for n, pair in enumerate(copies):
         for copy in pair:
             copy.wait()
         part = product_t(bras[n, :, :width], kets[n, 0])
         part = part + product_t(bras[n, :, width:], kets[n, 1])
-        if n > 0:
+        if n == 0:
+            total[...] = part
+        elif n < 7:
             total[...] += part
-        elif minus is None:
-            total[...] = part
+        elif turn == 0:
+            out[...] = (total[...] + part).astype(out.dtype)
         else:
-            total[...] = part - minus[...]
-    out[...] = total[...].astype(out.dtype)
+            last.wait()
+            out[...] = (total[...] + part) - less[...]
 
 
-def partial_sum(mine, other, ket, group, core, dtype, minus=None):
+def partial_sum(turn, where, mine, other, ket, *minus):
     rows, (blocks, columns, width) = mine.shape[1], ket.shape
-    where = jnp.stack([group * 4, core]).astype(jnp.int32)
     inside = pl.BlockSpec(memory_space=pltpu.VMEM)
     outside = pl.BlockSpec(memory_space=pltpu.HBM)
-    more = () if minus is None else (minus,)
+    scratch = [
+        pltpu.VMEM((8, rows, 2 * width), mine.dtype),
+        pltpu.VMEM((8, 2, columns, width), ket.dtype),
+        pltpu.VMEM((rows, columns), jnp.float32),
+        pltpu.SemaphoreType.DMA((2, 8)),
+    ]
+    if turn == 1:
+        scratch += [pltpu.VMEM((rows, columns), jnp.float32), pltpu.SemaphoreType.DMA]
     return pl.pallas_call(
-        sum_kernel,
-        out_shape=jax.ShapeDtypeStruct((rows, columns), dtype),
-        in_specs=[pl.BlockSpec(memory_space=pltpu.SMEM)] + [outside] * 3 + [inside] * len(more),
+        functools.partial(sum_kernel, turn),
+        out_shape=jax.ShapeDtypeStruct((rows, columns), (jnp.bfloat16, jnp.float32)[turn]),
+        in_specs=[pl.BlockSpec(memory_space=pltpu.SMEM)] + [outside] * (3 + len(minus)),
         out_specs=inside,
-        scratch_shapes=[
-            pltpu.VMEM((8, rows, 2 * width), mine.dtype),
-            pltpu.VMEM((8, 2, columns, width), ket.dtype),
-            pltpu.VMEM((rows, columns), jnp.float32),
-            pltpu.SemaphoreType.DMA((2, 8)),
-        ],
-        compiler_params=pltpu.CompilerParams(vmem_limit_bytes=56 * 1024 * 1024),
+        scratch_shapes=scratch,
+        compiler_params=pltpu.CompilerParams(vmem_limit_bytes=(56, 50)[turn] * 1024 * 1024),
         cost_estimate=pl.CostEstimate(
             flops=2 * rows * columns * blocks * width,
             bytes_accessed=2 * (rows + columns) * blocks * width,
             transcendentals=0,
         ),
-    )(where, mine, other, ket, *more)
+    )(where, mine, other, ket, *minus)
 
 
 def local(bra_density, ket_density, coulomb, cond_pairs, val_pairs, screened, q_owner, g_shift):
@@ -146,10 +157,11 @@
     direct = jnp.einsum("xcg,vug->vxuc", conds, pairs, preferred_element_type=jnp.float32)
 
     direct = direct.reshape(nv_size * cb_size, vb_size * nc_size)
-    direct, ket = lax.optimization_barrier((direct, ket))
-    send = partial_sum(mine, other, ket, 1 - ylo, core, jnp.bfloat16)
+    where = jnp.stack([4 - 4 * ylo, 4 * ylo, core]).astype(jnp.int32)
+    direct, ket, where = lax.optimization_barrier((direct, ket, where))
+    send = partial_sum(0, where, mine, other, ket)
     got = permute(send, lambda yl, zz, x, yh, c: (1 - yl, zz, x, yh, c))
-    keep = partial_sum(mine, other, ket, ylo, core, jnp.float32, direct)
+    keep = partial_sum(1, where, mine, other, ket, direct)
     return keep + got.astype(jnp.float32)
 
 

time: 127 us -> 124 us (0.976)
  other arithmetic: 4.06 us -> 2.43 us
  waiting for transfers between devices: 12.3 us -> 13.7 us
  Pallas kernels: 12 us -> 10.7 us
    pallas_call x2, Pallas kernels: 12 us -> 10.7 us  [partial_sum(): pl.pallas_call(functools.partial(sum_kernel, turn), out_shape=jax.ShapeDt...]
  transfers between devices with their start and end apart: 7 -> 7, of which waited for: 5 -> 6; matrix products, arithmetic and copies ran while one was open for 14% -> 13% of each run, Pallas kernels for 5% -> 4%
where the time goes in v2:
time: 124 us; the launch traced here: 123 us
  blocking collectives  42.4 us (34%)
  starting transfers between devices  23.8 us (19%)
  between operations  15.9 us (13%)
  waiting for transfers between devices  13.7 us (11%)
  local copies, waits for them, and re-layouts  11.6 us (9%)
  Pallas kernels  10.7 us (9%)
  matrix products  2.95 us (2%)
  other arithmetic  2.43 us (2%)
    all_to_all x1, blocking collectives, local(): mine = lax.all_to_all(spread, ('x', 'yhi'), 0, 0, tiled=True)  42.4 us
    ppermute x5, starting transfers between devices, permute(): return lax.ppermute(array, AXES, pairs)  14.5 us
    pallas_call x2, Pallas kernels, partial_sum(): pl.pallas_call(functools.partial(sum_kernel, turn), out_shape=jax.ShapeDt...  10.7 us
    all_to_all x1, starting transfers between devices, local(): lax.all_to_all(jnp.broadcast_to(w_half[None], (8,) + w_half.shape), ('x',...  9.28 us
    ppermute x5, waiting for transfers between devices, permute(): return lax.ppermute(array, AXES, pairs)  6.58 us
    gather x2, local copies, waits for them, and re-layouts, local(): shifted = jnp.take(vals, perm, axis=2).reshape(nv_size * vb_size, ngw_size)  4.24 us
    all_gather x1, waiting for transfers between devices, local(): ket = lax.all_gather(ket_density, 'z', axis=0)  3.78 us
    dot_general x1, matrix products, local(): jnp.einsum('xcg,vug->vxuc', conds, pairs, preferred_element_type=jnp.floa...  2.69 us
  transfers between devices with their start and end apart: 7, of which 6 were waited for; matrix products, arithmetic and copies ran while one was open for 13% of the time, Pallas kernels for 4%

profile of v2, /device:TPU:6, one launch (start us, length us, event | category | flops | bytes accessed | tf_op | source)
XLA Modules:
  0.0 123.4 jit_solution(841249859484045313)
XLA Ops:
  7.3 0.8 dynamic-slice_bitcast_fusion.1
  8.1 0.9 broadcast_in_dim.27
  9.0 9.3 %all-to-all-start = ((bf16[8,256,128]{2,1,0:T(8,128)(2,1)}), bf16[8,256,128]{2,1,0:T(8,128)(2,1)S(1)}, u32[]{:S(2)}, u32[]{:S(2)}) async-start(bf16[8,256,128]{2,1,0:T(8,128)(2,1)} %broadcast_in_dim.27), calls=%async_computation | async-start | bytes 1048576 | tf_op jit(solution)/shard_map/all_to_all | solution.py:131
  18.3 0.8 dynamic_slice.25
  19.1 1.9 %collective-permute-start = (bf16[256,768]{1,0:T(8,128)(2,1)S(1)}, bf16[256,768]{1,0:T(8,128)(2,1)S(1)}, u32[]{:S(2)}, u32[]{:S(2)}) collective-permute-start(bf16[256,768]{1,0:T(8,128)(2,1)S(1)} %fusion), channel_id=1, source_target_pairs={{0,0},{1,1},{2,2},{3,3},{4,4},{5,5},{6,6},{7,7},{8,256},{9,257},{1... | collective-permute-start | bytes 1179656 | tf_op jit(solution)/shard_map/ppermute | solution.py:32
  21.1 1.3 %dynamic_slice.26 = s32[1,1]{1,0:T(1,128)} dynamic-slice(s32[8,8]{1,0:T(8,128)} %param.14, s32[]{:T(128)S(6)} %select_n.87, s32[]{:T(128)S(6)} %select_n.89), dynamic_slice_sizes={1,1} | dynamic-slice | bytes 12 | tf_op jit(solution)/shard_map/dynamic_slice | solution.py:129
  24.6 2.6 %all-to-all-done = bf16[8,256,128]{2,1,0:T(8,128)(2,1)S(1)} async-done(((bf16[8,256,128]{2,1,0:T(8,128)(2,1)}), bf16[8,256,128]{2,1,0:T(8,128)(2,1)S(1)}, u32[]{:S(2)}, u32[]{:S(2)}) %all-to-all-start) | async-done | bytes 524320 | tf_op jit(solution)/shard_map/all_to_all | solution.py:131
  27.3 1.9 %collective-permute-start.1 = (bf16[256,128]{1,0:T(8,128)(2,1)S(1)}, bf16[256,128]{1,0:T(8,128)(2,1)S(1)}, u32[]{:S(2)}, u32[]{:S(2)}) collective-permute-start(bf16[256,128]{1,0:T(8,128)(2,1)S(1)} %dynamic-slice_bitcast_fusion), channel_id=1, source_target_pairs={{0,1},{1,0},{2,3},{3,2},{4,5},{5,4},{6,7},{7,6},{8,9},{9,8},{10,11... | collective-permute-start | bytes 196616 | tf_op jit(solution)/shard_map/ppermute | solution.py:32
  29.2 1.2 collective-permute-done.1
  30.4 1.9 %collective-permute-done = bf16[256,768]{1,0:T(8,128)(2,1)S(1)} collective-permute-done((bf16[256,768]{1,0:T(8,128)(2,1)S(1)}, bf16[256,768]{1,0:T(8,128)(2,1)S(1)}, u32[]{:S(2)}, u32[]{:S(2)}) %collective-permute-start) | collective-permute-done | bytes 393248 | tf_op jit(solution)/shard_map/ppermute | solution.py:32
  32.6 42.4 %all_to_all.10.mine = bf16[8,256,768]{2,1,0:T(8,128)(2,1)} all-to-all(bf16[8,256,768]{2,1,0:T(8,128)(2,1)S(1)} %broadcast_in_dim.28), channel_id=1, replica_groups=mesh['ylo'=2,'z'=16,'x'=4,'yhi'=2,'core'=2] {'x','yhi'}, dimensions={0} | all-to-all | bytes 6291456 | tf_op jit(solution)/shard_map/all_to_all | solution.py:141
  74.9 1.9 %collective-permute-start.3 = (bf16[8,256,768]{2,1,0:T(8,128)(2,1)}, bf16[8,256,768]{2,1,0:T(8,128)(2,1)}, u32[]{:S(2)}, u32[]{:S(2)}) collective-permute-start(bf16[8,256,768]{2,1,0:T(8,128)(2,1)} %all_to_all.10.mine), channel_id=1, source_target_pairs={{0,1},{1,0},{2,3},{3,2},{4,5},{5,4},{6,7},{7,6},{8,9},{9,8},{10,11... | collective-permute-start | bytes 9437192 | tf_op jit(solution)/shard_map/ppermute | solution.py:32
  77.6 5.3 %collective-permute-start.2 = (bf16[256,128]{1,0:T(8,128)(2,1)S(1)}, bf16[256,128]{1,0:T(8,128)(2,1)S(1)}, u32[]{:S(2)}, u32[]{:S(2)}) collective-permute-start(bf16[256,128]{1,0:T(8,128)(2,1)S(1)} %broadcast_select_fusion.2), channel_id=1, source_target_pairs={{0,16},{1,17},{2,18},{3,19},{4,20},{5,21},{6,22},{7,23},{8,24},{9,... | collective-permute-start | bytes 196616 | tf_op jit(solution)/shard_map/ppermute | solution.py:32
  83.6 3.4 %collective-permute-done.2 = bf16[256,128]{1,0:T(8,128)(2,1)S(1)} collective-permute-done((bf16[256,128]{1,0:T(8,128)(2,1)S(1)}, bf16[256,128]{1,0:T(8,128)(2,1)S(1)}, u32[]{:S(2)}, u32[]{:S(2)}) %collective-permute-start.2) | collective-permute-done | bytes 65568 | tf_op jit(solution)/shard_map/ppermute | solution.py:32
  87.0 1.0 copy.10
  88.0 1.8 %gather_fusion = bf16[256,32,16]{1,2,0:T(8,128)(2,1)} fusion(bf16[32,16,256]{0,1,2:T(8,128)(2,1)S(1)} %bitcast.36, s32[1024]{0:T(1024)S(1)} %pad_clamp_fusion), kind=kCustom, calls=%fused_computation | custom fusion | bytes 525312 | tf_op jit(solution)/shard_map/jit(_take)/gather | solution.py:151
  89.9 2.4 %copy.11 = bf16[32,16,256]{2,1,0:T(8,128)(2,1)S(1)} copy(bf16[32,16,256]{0,1,2:T(8,128)(2,1)} %bitcast.37) | data formatting | bytes 524288 | tf_op jit(solution)/shard_map/jit(_take)/gather | solution.py:151
  92.6 2.7 %convolution_bitcast_fusion = f32[32,8,16,32]{3,2,1,0:T(8,128)} fusion(bf16[32,16,256,1]{2,1,3,0:T(8,128)(2,1)S(1)} %bitcast.38, bf16[8,8,32,256]{3,2,1,0:T(8,128)(2,1)} %param.11, s32[]{:T(128)S(6)} %select_n.89), kind=kOutput, calls=%fused_computation.1 | convolution fusion | flops 67108864 | bytes 917508 | tf_op jit(solution)/shard_map/xcg,vug->vxuc/dot_general | solution.py:157
  95.3 2.3 %reshape.47.refs_0_ = f32[256,512]{1,0:T(8,128)S(1)} reshape(f32[32,8,16,32]{3,2,1,0:T(8,128)} %convolution_bitcast_fusion) | data formatting | bytes 1048576 | tf_op jit(solution)/shard_map/reshape | solution.py:159
  97.6 3.8 %all-gather.3.cloned.1.call-done = bf16[8192,384]{1,0:T(8,128)(2,1)} async-done(((bf16[512,384]{1,0:T(8,128)(2,1)}), bf16[8192,384]{1,0:T(8,128)(2,1)}) %all-gather.3.cloned.1.call-update) | async-done | bytes 6291472 | tf_op jit(solution)/shard_map/all_gather | solution.py:123
  101.4 5.8 %shard_map.83 = bf16[256,512]{1,0:T(8,128)(2,1)} custom-call(s32[3]{0:T(128)} %pad_add_fusion.where, bf16[8,256,768]{2,1,0:T(8,128)(2,1)} %all_to_all.10.mine, bf16[8,256,768]{2,1,0:T(8,128)(2,1)} %collective-permute-done.3.other, bf16[16,512,384]{2,1,0:T(8,128)(2,1)} %bitcast.34), custom_call_target="tpu_custom_call" | custom-call | flops 1610612736 | bytes 9437184 | tf_op jit(solution)/shard_map/pallas_call | solution.py:92
  107.2 3.4 %collective-permute-start.4 = (bf16[256,512]{1,0:T(8,128)(2,1)}, bf16[256,512]{1,0:T(8,128)(2,1)S(1)}, u32[]{:S(2)}, u32[]{:S(2)}) collective-permute-start(bf16[256,512]{1,0:T(8,128)(2,1)} %shard_map.83), channel_id=1, source_target_pairs={{0,256},{1,257},{2,258},{3,259},{4,260},{5,261},{6,262},{7,263},{8... | collective-permute-start | bytes 786440 | tf_op jit(solution)/shard_map/ppermute | solution.py:32
  110.6 4.9 %shard_map.82 = f32[256,512]{1,0:T(8,128)S(1)} custom-call(s32[3]{0:T(128)S(1)} %copy-done.1, bf16[8,256,768]{2,1,0:T(8,128)(2,1)} %all_to_all.10.mine, bf16[8,256,768]{2,1,0:T(8,128)(2,1)} %collective-permute-done.3.other, bf16[16,512,384]{2,1,0:T(8,128)(2,1)} %bitcast.35, f32[256,512]{1,0:T(8,128)S(1)} %reshape.47.refs_0_), custom_call_target="tpu_custom_call" | custom-call | flops 1610612736 | bytes 9437184 | tf_op jit(solution)/shard_map/pallas_call | solution.py:92
  115.7 0.9 convert_add_fusion
  (22 shorter events, 2.8 us)
Async XLA Ops:
  6.5 80.4 %copy-start = (bf16[8,32,16,256]{3,2,1,0:T(8,128)(2,1)S(1)}, bf16[8,32,16,256]{3,2,1,0:T(8,128)(2,1)}, u32[]{:S(2)}) copy-start(bf16[8,32,16,256]{3,2,1,0:T(8,128)(2,1)} %param.12) | copy-start | bytes 6291460
  6.5 12.5 %copy-start.2 = (bf16[256,768]{1,0:T(8,128)(2,1)S(1)}, bf16[256,768]{1,0:T(8,128)(2,1)}, u32[]{:S(2)}) copy-start(bf16[256,768]{1,0:T(8,128)(2,1)} %param.8) | copy-start | bytes 1179652
  6.5 94.9 %all-gather.3.cloned.1.call-start = ((), (), s32[]{:S(2)}) async-start(), calls=%async_computation.2 | async-start | bytes 6684672 | tf_op jit(solution)/shard_map/all_gather | solution.py:123
  9.0 18.3 %all-to-all-start = ((bf16[8,256,128]{2,1,0:T(8,128)(2,1)}), bf16[8,256,128]{2,1,0:T(8,128)(2,1)S(1)}, u32[]{:S(2)}, u32[]{:S(2)}) async-start(bf16[8,256,128]{2,1,0:T(8,128)(2,1)} %broadcast_in_dim.27), calls=%async_computation | async-start | bytes 1048576 | tf_op jit(solution)/shard_map/all_to_all | solution.py:131
  19.1 13.2 %collective-permute-start = (bf16[256,768]{1,0:T(8,128)(2,1)S(1)}, bf16[256,768]{1,0:T(8,128)(2,1)S(1)}, u32[]{:S(2)}, u32[]{:S(2)}) collective-permute-start(bf16[256,768]{1,0:T(8,128)(2,1)S(1)} %fusion), channel_id=1, source_target_pairs={{0,0},{1,1},{2,2},{3,3},{4,4},{5,5},{6,6},{7,7},{8,256},{9,257},{1... | collective-permute-start | bytes 1179656 | tf_op jit(solution)/shard_map/ppermute | solution.py:32
  27.3 3.1 %collective-permute-start.1 = (bf16[256,128]{1,0:T(8,128)(2,1)S(1)}, bf16[256,128]{1,0:T(8,128)(2,1)S(1)}, u32[]{:S(2)}, u32[]{:S(2)}) collective-permute-start(bf16[256,128]{1,0:T(8,128)(2,1)S(1)} %dynamic-slice_bitcast_fusion), channel_id=1, source_target_pairs={{0,1},{1,0},{2,3},{3,2},{4,5},{5,4},{6,7},{7,6},{8,9},{9,8},{10,11... | collective-permute-start | bytes 196616 | tf_op jit(solution)/shard_map/ppermute | solution.py:32
  74.9 26.5 %collective-permute-start.3 = (bf16[8,256,768]{2,1,0:T(8,128)(2,1)}, bf16[8,256,768]{2,1,0:T(8,128)(2,1)}, u32[]{:S(2)}, u32[]{:S(2)}) collective-permute-start(bf16[8,256,768]{2,1,0:T(8,128)(2,1)} %all_to_all.10.mine), channel_id=1, source_target_pairs={{0,1},{1,0},{2,3},{3,2},{4,5},{5,4},{6,7},{7,6},{8,9},{9,8},{10,11... | collective-permute-start | bytes 9437192 | tf_op jit(solution)/shard_map/ppermute | solution.py:32
  77.6 9.4 %collective-permute-start.2 = (bf16[256,128]{1,0:T(8,128)(2,1)S(1)}, bf16[256,128]{1,0:T(8,128)(2,1)S(1)}, u32[]{:S(2)}, u32[]{:S(2)}) collective-permute-start(bf16[256,128]{1,0:T(8,128)(2,1)S(1)} %broadcast_select_fusion.2), channel_id=1, source_target_pairs={{0,16},{1,17},{2,18},{3,19},{4,20},{5,21},{6,22},{7,23},{8,24},{9,... | collective-permute-start | bytes 196616 | tf_op jit(solution)/shard_map/ppermute | solution.py:32
  101.4 9.2 %copy-start.1 = (s32[3]{0:T(128)S(1)}, s32[3]{0:T(128)}, u32[]{:S(2)}) copy-start(s32[3]{0:T(128)} %pad_add_fusion.where) | copy-start | bytes 40
  107.2 8.5 %collective-permute-start.4 = (bf16[256,512]{1,0:T(8,128)(2,1)}, bf16[256,512]{1,0:T(8,128)(2,1)S(1)}, u32[]{:S(2)}, u32[]{:S(2)}) collective-permute-start(bf16[256,512]{1,0:T(8,128)(2,1)} %shard_map.83), channel_id=1, source_target_pairs={{0,256},{1,257},{2,258},{3,259},{4,260},{5,261},{6,262},{7,263},{8... | collective-permute-start | bytes 786440 | tf_op jit(solution)/shard_map/ppermute | solution.py:32
Sparse Core Ops, SparseCore 0:
  9.4 91.9 all-gather.2

commit v3 on v2

--- a/solution.py
+++ b/solution.py
@@ -95,7 +95,7 @@
         in_specs=[pl.BlockSpec(memory_space=pltpu.SMEM)] + [outside] * (3 + len(minus)),
         out_specs=inside,
         scratch_shapes=scratch,
-        compiler_params=pltpu.CompilerParams(vmem_limit_bytes=(56, 50)[turn] * 1024 * 1024),
+        compiler_params=pltpu.CompilerParams(vmem_limit_bytes=50 * 1024 * 1024),
         cost_estimate=pl.CostEstimate(
             flops=2 * rows * columns * blocks * width,
             bytes_accessed=2 * (rows + columns) * blocks * width,

time: 124 us -> 123 us (level)
  transfers between devices with their start and end apart: 7 -> 7, of which waited for: 6 -> 5; matrix products, arithmetic and copies ran while one was open for 13% -> 13% of each run, Pallas kernels for 4% -> 4%
where the time goes in v3:
time: 123 us; the launch traced here: 122 us
  blocking collectives  42.4 us (34%)
  starting transfers between devices  23.8 us (19%)
  between operations  16.4 us (13%)
  waiting for transfers between devices  13.6 us (11%)
  local copies, waits for them, and re-layouts  11.7 us (10%)
  Pallas kernels  9.83 us (8%)
  matrix products  2.96 us (2%)
  other arithmetic  1.84 us (1%)
    all_to_all x1, blocking collectives, local(): mine = lax.all_to_all(spread, ('x', 'yhi'), 0, 0, tiled=True)  42.4 us
    ppermute x5, starting transfers between devices, permute(): return lax.ppermute(array, AXES, pairs)  14.5 us
    pallas_call x2, Pallas kernels, partial_sum(): pl.pallas_call(functools.partial(sum_kernel, turn), out_shape=jax.ShapeDt...  9.83 us
    all_to_all x1, starting transfers between devices, local(): lax.all_to_all(jnp.broadcast_to(w_half[None], (8,) + w_half.shape), ('x',...  9.28 us
    ppermute x5, waiting for transfers between devices, permute(): return lax.ppermute(array, AXES, pairs)  7.09 us
    gather x2, local copies, waits for them, and re-layouts, local(): shifted = jnp.take(vals, perm, axis=2).reshape(nv_size * vb_size, ngw_size)  4.24 us
    all_gather x1, waiting for transfers between devices, local(): ket = lax.all_gather(ket_density, 'z', axis=0)  3.76 us
    dot_general x1, matrix products, local(): jnp.einsum('xcg,vug->vxuc', conds, pairs, preferred_element_type=jnp.floa...  2.7 us
  transfers between devices with their start and end apart: 7, of which 5 were waited for; matrix products, arithmetic and copies ran while one was open for 13% of the time, Pallas kernels for 4%

profile of v3, /device:TPU:6, one launch (start us, length us, event | category | flops | bytes accessed | tf_op | source)
XLA Modules:
  0.0 122.4 jit_solution(11558954153604850587)
XLA Ops:
  7.3 0.8 dynamic-slice_bitcast_fusion.1
  8.1 0.9 broadcast_in_dim.27
  9.0 9.3 %all-to-all-start = ((bf16[8,256,128]{2,1,0:T(8,128)(2,1)}), bf16[8,256,128]{2,1,0:T(8,128)(2,1)S(1)}, u32[]{:S(2)}, u32[]{:S(2)}) async-start(bf16[8,256,128]{2,1,0:T(8,128)(2,1)} %broadcast_in_dim.27), calls=%async_computation | async-start | bytes 1048576 | tf_op jit(solution)/shard_map/all_to_all | solution.py:131
  18.3 0.8 dynamic_slice.25
  19.1 1.9 %collective-permute-start = (bf16[256,768]{1,0:T(8,128)(2,1)S(1)}, bf16[256,768]{1,0:T(8,128)(2,1)S(1)}, u32[]{:S(2)}, u32[]{:S(2)}) collective-permute-start(bf16[256,768]{1,0:T(8,128)(2,1)S(1)} %fusion), channel_id=1, source_target_pairs={{0,0},{1,1},{2,2},{3,3},{4,4},{5,5},{6,6},{7,7},{8,256},{9,257},{1... | collective-permute-start | bytes 1179656 | tf_op jit(solution)/shard_map/ppermute | solution.py:32
  21.1 1.4 %dynamic_slice.26 = s32[1,1]{1,0:T(1,128)} dynamic-slice(s32[8,8]{1,0:T(8,128)} %param.14, s32[]{:T(128)S(6)} %select_n.87, s32[]{:T(128)S(6)} %select_n.89), dynamic_slice_sizes={1,1} | dynamic-slice | bytes 12 | tf_op jit(solution)/shard_map/dynamic_slice | solution.py:129
  25.3 2.0 %all-to-all-done = bf16[8,256,128]{2,1,0:T(8,128)(2,1)S(1)} async-done(((bf16[8,256,128]{2,1,0:T(8,128)(2,1)}), bf16[8,256,128]{2,1,0:T(8,128)(2,1)S(1)}, u32[]{:S(2)}, u32[]{:S(2)}) %all-to-all-start) | async-done | bytes 524320 | tf_op jit(solution)/shard_map/all_to_all | solution.py:131
  27.3 1.9 %collective-permute-start.1 = (bf16[256,128]{1,0:T(8,128)(2,1)S(1)}, bf16[256,128]{1,0:T(8,128)(2,1)S(1)}, u32[]{:S(2)}, u32[]{:S(2)}) collective-permute-start(bf16[256,128]{1,0:T(8,128)(2,1)S(1)} %dynamic-slice_bitcast_fusion), channel_id=1, source_target_pairs={{0,1},{1,0},{2,3},{3,2},{4,5},{5,4},{6,7},{7,6},{8,9},{9,8},{10,11... | collective-permute-start | bytes 196616 | tf_op jit(solution)/shard_map/ppermute | solution.py:32
  29.2 1.2 collective-permute-done.1
  30.4 1.9 %collective-permute-done = bf16[256,768]{1,0:T(8,128)(2,1)S(1)} collective-permute-done((bf16[256,768]{1,0:T(8,128)(2,1)S(1)}, bf16[256,768]{1,0:T(8,128)(2,1)S(1)}, u32[]{:S(2)}, u32[]{:S(2)}) %collective-permute-start) | collective-permute-done | bytes 393248 | tf_op jit(solution)/shard_map/ppermute | solution.py:32
  32.6 42.4 %all_to_all.10.mine = bf16[8,256,768]{2,1,0:T(8,128)(2,1)} all-to-all(bf16[8,256,768]{2,1,0:T(8,128)(2,1)S(1)} %broadcast_in_dim.28), channel_id=1, replica_groups=mesh['ylo'=2,'z'=16,'x'=4,'yhi'=2,'core'=2] {'x','yhi'}, dimensions={0} | all-to-all | bytes 6291456 | tf_op jit(solution)/shard_map/all_to_all | solution.py:141
  74.9 1.9 %collective-permute-start.3 = (bf16[8,256,768]{2,1,0:T(8,128)(2,1)}, bf16[8,256,768]{2,1,0:T(8,128)(2,1)}, u32[]{:S(2)}, u32[]{:S(2)}) collective-permute-start(bf16[8,256,768]{2,1,0:T(8,128)(2,1)} %all_to_all.10.mine), channel_id=1, source_target_pairs={{0,1},{1,0},{2,3},{3,2},{4,5},{5,4},{6,7},{7,6},{8,9},{9,8},{10,11... | collective-permute-start | bytes 9437192 | tf_op jit(solution)/shard_map/ppermute | solution.py:32
  77.6 5.3 %collective-permute-start.2 = (bf16[256,128]{1,0:T(8,128)(2,1)S(1)}, bf16[256,128]{1,0:T(8,128)(2,1)S(1)}, u32[]{:S(2)}, u32[]{:S(2)}) collective-permute-start(bf16[256,128]{1,0:T(8,128)(2,1)S(1)} %broadcast_select_fusion.2), channel_id=1, source_target_pairs={{0,16},{1,17},{2,18},{3,19},{4,20},{5,21},{6,22},{7,23},{8,24},{9,... | collective-permute-start | bytes 196616 | tf_op jit(solution)/shard_map/ppermute | solution.py:32
  83.0 3.9 %collective-permute-done.2 = bf16[256,128]{1,0:T(8,128)(2,1)S(1)} collective-permute-done((bf16[256,128]{1,0:T(8,128)(2,1)S(1)}, bf16[256,128]{1,0:T(8,128)(2,1)S(1)}, u32[]{:S(2)}, u32[]{:S(2)}) %collective-permute-start.2) | collective-permute-done | bytes 65568 | tf_op jit(solution)/shard_map/ppermute | solution.py:32
  87.0 1.1 copy.10
  88.0 1.8 %gather_fusion = bf16[256,32,16]{1,2,0:T(8,128)(2,1)} fusion(bf16[32,16,256]{0,1,2:T(8,128)(2,1)S(1)} %bitcast.36, s32[1024]{0:T(1024)S(1)} %pad_clamp_fusion), kind=kCustom, calls=%fused_computation | custom fusion | bytes 525312 | tf_op jit(solution)/shard_map/jit(_take)/gather | solution.py:151
  89.9 2.4 %copy.11 = bf16[32,16,256]{2,1,0:T(8,128)(2,1)S(1)} copy(bf16[32,16,256]{0,1,2:T(8,128)(2,1)} %bitcast.37) | data formatting | bytes 524288 | tf_op jit(solution)/shard_map/jit(_take)/gather | solution.py:151
  92.6 2.7 %convolution_bitcast_fusion = f32[32,8,16,32]{3,2,1,0:T(8,128)} fusion(bf16[32,16,256,1]{2,1,3,0:T(8,128)(2,1)S(1)} %bitcast.38, bf16[8,8,32,256]{3,2,1,0:T(8,128)(2,1)} %param.11, s32[]{:T(128)S(6)} %select_n.89), kind=kOutput, calls=%fused_computation.1 | convolution fusion | flops 67108864 | bytes 917508 | tf_op jit(solution)/shard_map/xcg,vug->vxuc/dot_general | solution.py:157
  95.3 2.3 %reshape.47.refs_0_ = f32[256,512]{1,0:T(8,128)S(1)} reshape(f32[32,8,16,32]{3,2,1,0:T(8,128)} %convolution_bitcast_fusion) | data formatting | bytes 1048576 | tf_op jit(solution)/shard_map/reshape | solution.py:159
  97.6 3.8 %all-gather.3.cloned.1.call-done = bf16[8192,384]{1,0:T(8,128)(2,1)} async-done(((bf16[512,384]{1,0:T(8,128)(2,1)}), bf16[8192,384]{1,0:T(8,128)(2,1)}) %all-gather.3.cloned.1.call-update) | async-done | bytes 6291472 | tf_op jit(solution)/shard_map/all_gather | solution.py:123
  101.4 4.9 %shard_map.83 = bf16[256,512]{1,0:T(8,128)(2,1)S(1)} custom-call(s32[3]{0:T(128)S(1)} %pad_add_fusion.where, bf16[8,256,768]{2,1,0:T(8,128)(2,1)} %all_to_all.10.mine, bf16[8,256,768]{2,1,0:T(8,128)(2,1)} %collective-permute-done.3.other, bf16[16,512,384]{2,1,0:T(8,128)(2,1)} %bitcast.34), custom_call_target="tpu_custom_call" | custom-call | flops 1610612736 | bytes 9437184 | tf_op jit(solution)/shard_map/pallas_call | solution.py:92
  106.3 3.4 %collective-permute-start.4 = (bf16[256,512]{1,0:T(8,128)(2,1)S(1)}, bf16[256,512]{1,0:T(8,128)(2,1)S(1)}, u32[]{:S(2)}, u32[]{:S(2)}) collective-permute-start(bf16[256,512]{1,0:T(8,128)(2,1)S(1)} %shard_map.83), channel_id=1, source_target_pairs={{0,256},{1,257},{2,258},{3,259},{4,260},{5,261},{6,262},{7,263},{8... | collective-permute-start | bytes 786440 | tf_op jit(solution)/shard_map/ppermute | solution.py:32
  109.7 4.9 %shard_map.82 = f32[256,512]{1,0:T(8,128)S(1)} custom-call(s32[3]{0:T(128)S(1)} %pad_add_fusion.where, bf16[8,256,768]{2,1,0:T(8,128)(2,1)} %all_to_all.10.mine, bf16[8,256,768]{2,1,0:T(8,128)(2,1)} %collective-permute-done.3.other, bf16[16,512,384]{2,1,0:T(8,128)(2,1)} %bitcast.35, f32[256,512]{1,0:T(8,128)S(1)} %reshape.47.refs_0_), custom_call_target="tpu_custom_call" | custom-call | flops 1610612736 | bytes 9437184 | tf_op jit(solution)/shard_map/pallas_call | solution.py:92
  114.7 0.9 convert_add_fusion
  (20 shorter events, 2.2 us)
Async XLA Ops:
  6.5 80.4 %copy-start = (bf16[8,32,16,256]{3,2,1,0:T(8,128)(2,1)S(1)}, bf16[8,32,16,256]{3,2,1,0:T(8,128)(2,1)}, u32[]{:S(2)}) copy-start(bf16[8,32,16,256]{3,2,1,0:T(8,128)(2,1)} %param.12) | copy-start | bytes 6291460
  6.5 12.5 %copy-start.1 = (bf16[256,768]{1,0:T(8,128)(2,1)S(1)}, bf16[256,768]{1,0:T(8,128)(2,1)}, u32[]{:S(2)}) copy-start(bf16[256,768]{1,0:T(8,128)(2,1)} %param.8) | copy-start | bytes 1179652
  6.5 94.9 %all-gather.3.cloned.1.call-start = ((), (), s32[]{:S(2)}) async-start(), calls=%async_computation.2 | async-start | bytes 6684672 | tf_op jit(solution)/shard_map/all_gather | solution.py:123
  9.0 18.3 %all-to-all-start = ((bf16[8,256,128]{2,1,0:T(8,128)(2,1)}), bf16[8,256,128]{2,1,0:T(8,128)(2,1)S(1)}, u32[]{:S(2)}, u32[]{:S(2)}) async-start(bf16[8,256,128]{2,1,0:T(8,128)(2,1)} %broadcast_in_dim.27), calls=%async_computation | async-start | bytes 1048576 | tf_op jit(solution)/shard_map/all_to_all | solution.py:131
  19.1 13.2 %collective-permute-start = (bf16[256,768]{1,0:T(8,128)(2,1)S(1)}, bf16[256,768]{1,0:T(8,128)(2,1)S(1)}, u32[]{:S(2)}, u32[]{:S(2)}) collective-permute-start(bf16[256,768]{1,0:T(8,128)(2,1)S(1)} %fusion), channel_id=1, source_target_pairs={{0,0},{1,1},{2,2},{3,3},{4,4},{5,5},{6,6},{7,7},{8,256},{9,257},{1... | collective-permute-start | bytes 1179656 | tf_op jit(solution)/shard_map/ppermute | solution.py:32
  27.3 3.1 %collective-permute-start.1 = (bf16[256,128]{1,0:T(8,128)(2,1)S(1)}, bf16[256,128]{1,0:T(8,128)(2,1)S(1)}, u32[]{:S(2)}, u32[]{:S(2)}) collective-permute-start(bf16[256,128]{1,0:T(8,128)(2,1)S(1)} %dynamic-slice_bitcast_fusion), channel_id=1, source_target_pairs={{0,1},{1,0},{2,3},{3,2},{4,5},{5,4},{6,7},{7,6},{8,9},{9,8},{10,11... | collective-permute-start | bytes 196616 | tf_op jit(solution)/shard_map/ppermute | solution.py:32
  74.9 26.5 %collective-permute-start.3 = (bf16[8,256,768]{2,1,0:T(8,128)(2,1)}, bf16[8,256,768]{2,1,0:T(8,128)(2,1)}, u32[]{:S(2)}, u32[]{:S(2)}) collective-permute-start(bf16[8,256,768]{2,1,0:T(8,128)(2,1)} %all_to_all.10.mine), channel_id=1, source_target_pairs={{0,1},{1,0},{2,3},{3,2},{4,5},{5,4},{6,7},{7,6},{8,9},{9,8},{10,11... | collective-permute-start | bytes 9437192 | tf_op jit(solution)/shard_map/ppermute | solution.py:32
  77.6 9.4 %collective-permute-start.2 = (bf16[256,128]{1,0:T(8,128)(2,1)S(1)}, bf16[256,128]{1,0:T(8,128)(2,1)S(1)}, u32[]{:S(2)}, u32[]{:S(2)}) collective-permute-start(bf16[256,128]{1,0:T(8,128)(2,1)S(1)} %broadcast_select_fusion.2), channel_id=1, source_target_pairs={{0,16},{1,17},{2,18},{3,19},{4,20},{5,21},{6,22},{7,23},{8,24},{9,... | collective-permute-start | bytes 196616 | tf_op jit(solution)/shard_map/ppermute | solution.py:32
  106.3 8.4 %collective-permute-start.4 = (bf16[256,512]{1,0:T(8,128)(2,1)S(1)}, bf16[256,512]{1,0:T(8,128)(2,1)S(1)}, u32[]{:S(2)}, u32[]{:S(2)}) collective-permute-start(bf16[256,512]{1,0:T(8,128)(2,1)S(1)} %shard_map.83), channel_id=1, source_target_pairs={{0,256},{1,257},{2,258},{3,259},{4,260},{5,261},{6,262},{7,263},{8... | collective-permute-start | bytes 786440 | tf_op jit(solution)/shard_map/ppermute | solution.py:32
Sparse Core Ops, SparseCore 0:
  9.4 91.9 all-gather.2

commit v4 on v3

--- a/solution.py
+++ b/solution.py
@@ -136,7 +136,7 @@
     w_mine = jnp.where(q_index % 2 == core, w_mine, w_other)
     w_other = permute(w_mine, lambda yl, zz, x, yh, c: (yl, zz ^ 1, x, yh, c))
 
-    moved, w_mine = lax.optimization_barrier((moved, w_mine))
+    moved, w_mine, w_other = lax.optimization_barrier((moved, w_mine, w_other))
     spread = jnp.broadcast_to(moved[None], (8,) + moved.shape)
     mine = lax.all_to_all(spread, ("x", "yhi"), 0, 0, tiled=True)
     other = permute(mine, lambda yl, zz, x, yh, c: (yl, zz, x, yh, 1 - c))

time: 123 us -> 123 us (level)
  starting transfers between devices: 23.8 us -> 20.3 us
  waiting for transfers between devices: 13.6 us -> 16.9 us
    ppermute x5, starting transfers between devices: 14.5 us -> 11 us  [permute(): return lax.ppermute(array, AXES, pairs)]
    all_gather x1, waiting for transfers between devices: 3.76 us -> 6.99 us  [local(): ket = lax.all_gather(ket_density, 'z', axis=0)]
where the time goes in v4:
time: 123 us
  blocking collectives  42.7 us (35%)
  starting transfers between devices  20.3 us (17%)
  waiting for transfers between devices  16.9 us (14%)
  between operations  16.4 us (13%)
  local copies, waits for them, and re-layouts  11.7 us (10%)
  Pallas kernels  9.83 us (8%)
  matrix products  2.95 us (2%)
  other arithmetic  1.83 us (1%)
    all_to_all x1, blocking collectives, local(): mine = lax.all_to_all(spread, ('x', 'yhi'), 0, 0, tiled=True)  42.7 us
    ppermute x5, starting transfers between devices, permute(): return lax.ppermute(array, AXES, pairs)  11 us
    pallas_call x2, Pallas kernels, partial_sum(): pl.pallas_call(functools.partial(sum_kernel, turn), out_shape=jax.ShapeDt...  9.83 us
    all_to_all x1, starting transfers between devices, local(): lax.all_to_all(jnp.broadcast_to(w_half[None], (8,) + w_half.shape), ('x',...  9.28 us
    ppermute x5, waiting for transfers between devices, permute(): return lax.ppermute(array, AXES, pairs)  7.15 us
    all_gather x1, waiting for transfers between devices, local(): ket = lax.all_gather(ket_density, 'z', axis=0)  6.99 us
    gather x2, local copies, waits for them, and re-layouts, local(): shifted = jnp.take(vals, perm, axis=2).reshape(nv_size * vb_size, ngw_size)  4.26 us
    dot_general x1, matrix products, local(): jnp.einsum('xcg,vug->vxuc', conds, pairs, preferred_element_type=jnp.floa...  2.7 us
  transfers between devices with their start and end apart: 7, of which 5 were waited for; matrix products, arithmetic and copies ran while one was open for 13% of the time, Pallas kernels for 4%

profile of v4, /device:TPU:6, one launch (start us, length us, event | category | flops | bytes accessed | tf_op | source)
XLA Modules:
  0.0 122.6 jit_solution(17060060926621587244)
XLA Ops:
  6.5 0.7 all-gather.3.cloned.1.call-update
  7.3 0.8 dynamic-slice_bitcast_fusion.1
  8.1 0.9 broadcast_in_dim.27
  9.0 9.3 %all-to-all-start = ((bf16[8,256,128]{2,1,0:T(8,128)(2,1)}), bf16[8,256,128]{2,1,0:T(8,128)(2,1)S(1)}, u32[]{:S(2)}, u32[]{:S(2)}) async-start(bf16[8,256,128]{2,1,0:T(8,128)(2,1)} %broadcast_in_dim.27), calls=%async_computation | async-start | bytes 1048576 | tf_op jit(solution)/shard_map/all_to_all | solution.py:131
  18.3 0.8 dynamic_slice.25
  19.1 1.9 %collective-permute-start = (bf16[256,768]{1,0:T(8,128)(2,1)S(1)}, bf16[256,768]{1,0:T(8,128)(2,1)S(1)}, u32[]{:S(2)}, u32[]{:S(2)}) collective-permute-start(bf16[256,768]{1,0:T(8,128)(2,1)S(1)} %fusion), channel_id=1, source_target_pairs={{0,0},{1,1},{2,2},{3,3},{4,4},{5,5},{6,6},{7,7},{8,256},{9,257},{1... | collective-permute-start | bytes 1179656 | tf_op jit(solution)/shard_map/ppermute | solution.py:32
  21.1 1.4 %dynamic_slice.26 = s32[1,1]{1,0:T(1,128)} dynamic-slice(s32[8,8]{1,0:T(8,128)} %param.14, s32[]{:T(128)S(6)} %select_n.87, s32[]{:T(128)S(6)} %select_n.89), dynamic_slice_sizes={1,1} | dynamic-slice | bytes 12 | tf_op jit(solution)/shard_map/dynamic_slice | solution.py:129
  25.3 2.0 %all-to-all-done = bf16[8,256,128]{2,1,0:T(8,128)(2,1)S(1)} async-done(((bf16[8,256,128]{2,1,0:T(8,128)(2,1)}), bf16[8,256,128]{2,1,0:T(8,128)(2,1)S(1)}, u32[]{:S(2)}, u32[]{:S(2)}) %all-to-all-start) | async-done | bytes 524320 | tf_op jit(solution)/shard_map/all_to_all | solution.py:131
  27.3 1.9 %collective-permute-start.1 = (bf16[256,128]{1,0:T(8,128)(2,1)S(1)}, bf16[256,128]{1,0:T(8,128)(2,1)S(1)}, u32[]{:S(2)}, u32[]{:S(2)}) collective-permute-start(bf16[256,128]{1,0:T(8,128)(2,1)S(1)} %dynamic-slice_bitcast_fusion), channel_id=1, source_target_pairs={{0,1},{1,0},{2,3},{3,2},{4,5},{5,4},{6,7},{7,6},{8,9},{9,8},{10,11... | collective-permute-start | bytes 196616 | tf_op jit(solution)/shard_map/ppermute | solution.py:32
  29.2 1.2 collective-permute-done.1
  30.4 2.2 %collective-permute-start.2 = (bf16[256,128]{1,0:T(8,128)(2,1)S(1)}, bf16[256,128]{1,0:T(8,128)(2,1)S(1)}, u32[]{:S(2)}, u32[]{:S(2)}) collective-permute-start(bf16[256,128]{1,0:T(8,128)(2,1)S(1)} %broadcast_select_fusion.2), channel_id=1, source_target_pairs={{0,16},{1,17},{2,18},{3,19},{4,20},{5,21},{6,22},{7,23},{8,24},{9,... | collective-permute-start | bytes 196616 | tf_op jit(solution)/shard_map/ppermute | solution.py:32
  32.7 5.7 %collective-permute-done.2 = bf16[256,128]{1,0:T(8,128)(2,1)S(1)} collective-permute-done((bf16[256,128]{1,0:T(8,128)(2,1)S(1)}, bf16[256,128]{1,0:T(8,128)(2,1)S(1)}, u32[]{:S(2)}, u32[]{:S(2)}) %collective-permute-start.2) | collective-permute-done | bytes 65568 | tf_op jit(solution)/shard_map/ppermute | solution.py:32
  38.6 42.7 %all_to_all.10.mine = bf16[8,256,768]{2,1,0:T(8,128)(2,1)} all-to-all(bf16[8,256,768]{2,1,0:T(8,128)(2,1)S(1)} %broadcast_in_dim.28), channel_id=1, replica_groups=mesh['ylo'=2,'z'=16,'x'=4,'yhi'=2,'core'=2] {'x','yhi'}, dimensions={0} | all-to-all | bytes 6291456 | tf_op jit(solution)/shard_map/all_to_all | solution.py:141
  81.3 1.9 %collective-permute-start.3 = (bf16[8,256,768]{2,1,0:T(8,128)(2,1)}, bf16[8,256,768]{2,1,0:T(8,128)(2,1)}, u32[]{:S(2)}, u32[]{:S(2)}) collective-permute-start(bf16[8,256,768]{2,1,0:T(8,128)(2,1)} %all_to_all.10.mine), channel_id=1, source_target_pairs={{0,1},{1,0},{2,3},{3,2},{4,5},{5,4},{6,7},{7,6},{8,9},{9,8},{10,11... | collective-permute-start | bytes 9437192 | tf_op jit(solution)/shard_map/ppermute | solution.py:32
  84.0 1.1 copy.10
  85.1 1.8 %gather_fusion = bf16[256,32,16]{1,2,0:T(8,128)(2,1)} fusion(bf16[32,16,256]{0,1,2:T(8,128)(2,1)S(1)} %bitcast.36, s32[1024]{0:T(1024)S(1)} %pad_clamp_fusion), kind=kCustom, calls=%fused_computation | custom fusion | bytes 525312 | tf_op jit(solution)/shard_map/jit(_take)/gather | solution.py:151
  87.0 2.4 %copy.11 = bf16[32,16,256]{2,1,0:T(8,128)(2,1)S(1)} copy(bf16[32,16,256]{0,1,2:T(8,128)(2,1)} %bitcast.37) | data formatting | bytes 524288 | tf_op jit(solution)/shard_map/jit(_take)/gather | solution.py:151
  89.7 2.7 %convolution_bitcast_fusion = f32[32,8,16,32]{3,2,1,0:T(8,128)} fusion(bf16[32,16,256,1]{2,1,3,0:T(8,128)(2,1)S(1)} %bitcast.38, bf16[8,8,32,256]{3,2,1,0:T(8,128)(2,1)} %param.11, s32[]{:T(128)S(6)} %select_n.89), kind=kOutput, calls=%fused_computation.1 | convolution fusion | flops 67108864 | bytes 917508 | tf_op jit(solution)/shard_map/xcg,vug->vxuc/dot_general | solution.py:157
  92.4 2.3 %reshape.47.refs_0_ = f32[256,512]{1,0:T(8,128)S(1)} reshape(f32[32,8,16,32]{3,2,1,0:T(8,128)} %convolution_bitcast_fusion) | data formatting | bytes 1048576 | tf_op jit(solution)/shard_map/reshape | solution.py:159
  94.7 7.0 %all-gather.3.cloned.1.call-done = bf16[8192,384]{1,0:T(8,128)(2,1)} async-done(((bf16[512,384]{1,0:T(8,128)(2,1)}), bf16[8192,384]{1,0:T(8,128)(2,1)}) %all-gather.3.cloned.1.call-update) | async-done | bytes 6291472 | tf_op jit(solution)/shard_map/all_gather | solution.py:123
  101.7 4.9 %shard_map.83 = bf16[256,512]{1,0:T(8,128)(2,1)S(1)} custom-call(s32[3]{0:T(128)S(1)} %pad_add_fusion.where, bf16[8,256,768]{2,1,0:T(8,128)(2,1)} %all_to_all.10.mine, bf16[8,256,768]{2,1,0:T(8,128)(2,1)} %collective-permute-done.3.other, bf16[16,512,384]{2,1,0:T(8,128)(2,1)} %bitcast.34), custom_call_target="tpu_custom_call" | custom-call | flops 1610612736 | bytes 9437184 | tf_op jit(solution)/shard_map/pallas_call | solution.py:92
  106.6 3.1 %collective-permute-start.4 = (bf16[256,512]{1,0:T(8,128)(2,1)S(1)}, bf16[256,512]{1,0:T(8,128)(2,1)S(1)}, u32[]{:S(2)}, u32[]{:S(2)}) collective-permute-start(bf16[256,512]{1,0:T(8,128)(2,1)S(1)} %shard_map.83), channel_id=1, source_target_pairs={{0,256},{1,257},{2,258},{3,259},{4,260},{5,261},{6,262},{7,263},{8... | collective-permute-start | bytes 786440 | tf_op jit(solution)/shard_map/ppermute | solution.py:32
  109.7 4.9 %shard_map.82 = f32[256,512]{1,0:T(8,128)S(1)} custom-call(s32[3]{0:T(128)S(1)} %pad_add_fusion.where, bf16[8,256,768]{2,1,0:T(8,128)(2,1)} %all_to_all.10.mine, bf16[8,256,768]{2,1,0:T(8,128)(2,1)} %collective-permute-done.3.other, bf16[16,512,384]{2,1,0:T(8,128)(2,1)} %bitcast.35, f32[256,512]{1,0:T(8,128)S(1)} %reshape.47.refs_0_), custom_call_target="tpu_custom_call" | custom-call | flops 1610612736 | bytes 9437184 | tf_op jit(solution)/shard_map/pallas_call | solution.py:92
  114.9 0.9 convert_add_fusion
  (20 shorter events, 1.7 us)
Async XLA Ops:
  6.5 77.5 %copy-start = (bf16[8,32,16,256]{3,2,1,0:T(8,128)(2,1)S(1)}, bf16[8,32,16,256]{3,2,1,0:T(8,128)(2,1)}, u32[]{:S(2)}) copy-start(bf16[8,32,16,256]{3,2,1,0:T(8,128)(2,1)} %param.12) | copy-start | bytes 6291460
  6.5 12.5 %copy-start.1 = (bf16[256,768]{1,0:T(8,128)(2,1)S(1)}, bf16[256,768]{1,0:T(8,128)(2,1)}, u32[]{:S(2)}) copy-start(bf16[256,768]{1,0:T(8,128)(2,1)} %param.8) | copy-start | bytes 1179652
  6.5 95.2 %all-gather.3.cloned.1.call-start = ((), (), s32[]{:S(2)}) async-start(), calls=%async_computation.2 | async-start | bytes 6684672 | tf_op jit(solution)/shard_map/all_gather | solution.py:123
  9.0 18.3 %all-to-all-start = ((bf16[8,256,128]{2,1,0:T(8,128)(2,1)}), bf16[8,256,128]{2,1,0:T(8,128)(2,1)S(1)}, u32[]{:S(2)}, u32[]{:S(2)}) async-start(bf16[8,256,128]{2,1,0:T(8,128)(2,1)} %broadcast_in_dim.27), calls=%async_computation | async-start | bytes 1048576 | tf_op jit(solution)/shard_map/all_to_all | solution.py:131
  19.1 13.5 %collective-permute-start = (bf16[256,768]{1,0:T(8,128)(2,1)S(1)}, bf16[256,768]{1,0:T(8,128)(2,1)S(1)}, u32[]{:S(2)}, u32[]{:S(2)}) collective-permute-start(bf16[256,768]{1,0:T(8,128)(2,1)S(1)} %fusion), channel_id=1, source_target_pairs={{0,0},{1,1},{2,2},{3,3},{4,4},{5,5},{6,6},{7,7},{8,256},{9,257},{1... | collective-permute-start | bytes 1179656 | tf_op jit(solution)/shard_map/ppermute | solution.py:32
  27.3 3.1 %collective-permute-start.1 = (bf16[256,128]{1,0:T(8,128)(2,1)S(1)}, bf16[256,128]{1,0:T(8,128)(2,1)S(1)}, u32[]{:S(2)}, u32[]{:S(2)}) collective-permute-start(bf16[256,128]{1,0:T(8,128)(2,1)S(1)} %dynamic-slice_bitcast_fusion), channel_id=1, source_target_pairs={{0,1},{1,0},{2,3},{3,2},{4,5},{5,4},{6,7},{7,6},{8,9},{9,8},{10,11... | collective-permute-start | bytes 196616 | tf_op jit(solution)/shard_map/ppermute | solution.py:32
  30.4 8.0 %collective-permute-start.2 = (bf16[256,128]{1,0:T(8,128)(2,1)S(1)}, bf16[256,128]{1,0:T(8,128)(2,1)S(1)}, u32[]{:S(2)}, u32[]{:S(2)}) collective-permute-start(bf16[256,128]{1,0:T(8,128)(2,1)S(1)} %broadcast_select_fusion.2), channel_id=1, source_target_pairs={{0,16},{1,17},{2,18},{3,19},{4,20},{5,21},{6,22},{7,23},{8,24},{9,... | collective-permute-start | bytes 196616 | tf_op jit(solution)/shard_map/ppermute | solution.py:32
  81.3 20.5 %collective-permute-start.3 = (bf16[8,256,768]{2,1,0:T(8,128)(2,1)}, bf16[8,256,768]{2,1,0:T(8,128)(2,1)}, u32[]{:S(2)}, u32[]{:S(2)}) collective-permute-start(bf16[8,256,768]{2,1,0:T(8,128)(2,1)} %all_to_all.10.mine), channel_id=1, source_target_pairs={{0,1},{1,0},{2,3},{3,2},{4,5},{5,4},{6,7},{7,6},{8,9},{9,8},{10,11... | collective-permute-start | bytes 9437192 | tf_op jit(solution)/shard_map/ppermute | solution.py:32
  106.6 8.3 %collective-permute-start.4 = (bf16[256,512]{1,0:T(8,128)(2,1)S(1)}, bf16[256,512]{1,0:T(8,128)(2,1)S(1)}, u32[]{:S(2)}, u32[]{:S(2)}) collective-permute-start(bf16[256,512]{1,0:T(8,128)(2,1)S(1)} %shard_map.83), channel_id=1, source_target_pairs={{0,256},{1,257},{2,258},{3,259},{4,260},{5,261},{6,262},{7,263},{8... | collective-permute-start | bytes 786440 | tf_op jit(solution)/shard_map/ppermute | solution.py:32
Sparse Core Ops, SparseCore 0:
  9.4 92.2 all-gather.2
